TPU v7x, 512 devices: a whole 4x8x8 slice. The times are simulated.
512 devices in a mesh: expert: 32 (over y_hi, z), dp: 16 (over x, y_lo, core).
Axes of the slice: x: 4, y: 8 (y_hi: 4, y_lo: 2; y = y_hi * 2 + y_lo), z: 8, core: 2. Of those that a mesh axis runs over, the one named last changes fastest.
Arguments:
- tokens: bfloat16 [65536, 2560], P(('expert', 'dp')), may hold values from -6 to 6
- cotangent: bfloat16 [65536, 2560], P(('expert', 'dp')), may hold values from -6 to 6
- gates: bfloat16 [65536, 2], P(('expert', 'dp')), may hold values from 0.099609375 to 1
- routes: int32 [65536, 2], P(('expert', 'dp')), may hold values from -1 to 7, as said below
- gate_proj: bfloat16 [32, 192, 2560], P('expert', 'dp'), may hold values from -0.125 to 0.125
- up_proj: bfloat16 [32, 192, 2560], P('expert', 'dp'), may hold values from -0.125 to 0.125
- down_proj: bfloat16 [32, 192, 2560], P('expert', 'dp'), may hold values from -0.21875 to 0.21875
Outputs:
- grad_tokens: bfloat16 [65536, 2560], P(('expert', 'dp'))
- grad_gates: float32 [65536, 2], P(('expert', 'dp'))
- grad_gate_proj: bfloat16 [32, 192, 2560], P('expert', 'dp')
- grad_up_proj: bfloat16 [32, 192, 2560], P('expert', 'dp')
- grad_down_proj: bfloat16 [32, 192, 2560], P('expert', 'dp')
Inputs may be any that keep to these rules, and one draw needn't show every extreme that they name: `routes`: each row lists 1 to 2 different experts in its first entries and -1 in the others.
All inputs are finite; a program needn't handle non-finite values.
Results may differ from a plain program's by a relative error of at most 0.0085.
Values may be sent and summed in bfloat16 or wider, within the bound.
A program may use at most 64 MiB of HBM per device.

v0:
```python
import jax
import jax.numpy as jnp
from jax import lax
from jax.sharding import PartitionSpec as P

GROUP = 4


def slot_tables(route_block, experts, capacity):
    expert_range = jnp.arange(experts, dtype=jnp.int32)
    named = route_block[:, :, None] == expert_range[None, None, :]
    hits = jnp.sum(named.astype(jnp.int32), axis=1)
    before = jnp.cumsum(hits, axis=0) - hits
    rank_pick = jnp.sum(jnp.where(named, before[:, None, :], 0), axis=2)
    kept_slot = (route_block >= 0) & (rank_pick < capacity)
    slot_ids = jnp.where(kept_slot, route_block * capacity + rank_pick, -1)
    return slot_ids


def unit_pass(rows_x, scaled_dy, gate_rows, up_rows, down_rows):
    contract = (((1,), (1,)), ((), ()))
    pre_gate = lax.dot_general(rows_x, gate_rows, contract, preferred_element_type=jnp.float32)
    pre_up = lax.dot_general(rows_x, up_rows, contract, preferred_element_type=jnp.float32)
    sigmoid_gate = jax.nn.sigmoid(pre_gate)
    activated = pre_gate * sigmoid_gate
    hidden = (activated * pre_up).astype(jnp.bfloat16)
    outward = jnp.dot(hidden, down_rows, preferred_element_type=jnp.float32)
    grad_hidden = lax.dot_general(
        scaled_dy, down_rows, contract, preferred_element_type=jnp.float32
    )
    grad_pre_gate = (
        grad_hidden * pre_up * sigmoid_gate * (1.0 + pre_gate * (1.0 - sigmoid_gate))
    ).astype(jnp.bfloat16)
    grad_pre_up = (grad_hidden * activated).astype(jnp.bfloat16)
    slot_grad = jnp.dot(grad_pre_gate, gate_rows, preferred_element_type=jnp.float32) + jnp.dot(
        grad_pre_up, up_rows, preferred_element_type=jnp.float32
    )
    return (hidden, grad_pre_gate, grad_pre_up, outward, slot_grad)


def spread_out(buffer, experts, capacity):
    shaped = buffer.reshape((experts, 1, capacity) + buffer.shape[1:])
    copies = jnp.broadcast_to(shaped, (experts, GROUP, capacity) + buffer.shape[1:])
    return copies.reshape((experts * GROUP, capacity) + buffer.shape[1:])


def per_device(tokens, cotangent, gates, routes, gate_proj, up_proj, down_proj):
    tok_rows, model_width = tokens.shape
    members = lax.axis_size("expert")
    experts = members // GROUP
    capacity = max(2, tok_rows // experts)
    slot_count = experts * capacity
    slot_ids = slot_tables(routes, experts, capacity)
    slot_range = jnp.arange(slot_count, dtype=jnp.int32)
    picked = slot_ids[None, :, :] == slot_range[:, None, None]
    placing = jnp.any(picked, axis=2)
    place_bf = placing.astype(jnp.bfloat16)
    sent_x = jnp.dot(place_bf, tokens, preferred_element_type=jnp.float32).astype(jnp.bfloat16)
    sent_dy = jnp.dot(place_bf, cotangent, preferred_element_type=jnp.float32).astype(jnp.bfloat16)
    sent_gate = jnp.sum(
        jnp.where(picked, gates.astype(jnp.float32)[None, :, :], 0.0), axis=(1, 2)
    ).astype(jnp.bfloat16)
    got_x, got_dy, got_gate = (
        lax.all_to_all(
            spread_out(sent_x, experts, capacity), "expert", split_axis=0, concat_axis=0, tiled=True
        ),
        lax.all_to_all(
            spread_out(sent_dy, experts, capacity),
            "expert",
            split_axis=0,
            concat_axis=0,
            tiled=True,
        ),
        lax.all_to_all(
            spread_out(sent_gate, experts, capacity),
            "expert",
            split_axis=0,
            concat_axis=0,
            tiled=True,
        ),
    )
    rows_x = got_x.reshape(-1, model_width)
    rows_dy = got_dy.reshape(-1, model_width)
    rows_gate = got_gate.reshape(-1).astype(jnp.float32)
    scaled_dy = (rows_gate[:, None] * rows_dy.astype(jnp.float32)).astype(jnp.bfloat16)
    full_gate, full_up, full_down = (
        lax.all_gather(gate_proj, "dp", axis=1, tiled=True),
        lax.all_gather(up_proj, "dp", axis=1, tiled=True),
        lax.all_gather(down_proj, "dp", axis=1, tiled=True),
    )
    hidden, grad_pre_gate, grad_pre_up, outward, slot_grad = unit_pass(
        rows_x, scaled_dy, full_gate[0], full_up[0], full_down[0]
    )
    gate_part = jnp.sum(rows_dy.astype(jnp.float32) * outward, axis=1).astype(jnp.bfloat16)
    slot_part = slot_grad.astype(jnp.bfloat16)
    contract_rows = (((0,), (0,)), ((), ()))
    term_gate = lax.dot_general(
        grad_pre_gate, rows_x, contract_rows, preferred_element_type=jnp.float32
    )
    term_up = lax.dot_general(
        grad_pre_up, rows_x, contract_rows, preferred_element_type=jnp.float32
    )
    term_down = lax.dot_general(
        hidden, scaled_dy, contract_rows, preferred_element_type=jnp.float32
    )
    whole_term = jnp.stack([term_gate, term_up, term_down], axis=1).astype(jnp.bfloat16)
    parted = whole_term.reshape(lax.axis_size("dp"), gate_proj.shape[1], 3, model_width)
    swapped = lax.all_to_all(parted, "dp", split_axis=0, concat_axis=0, tiled=True)
    shares = jnp.sum(swapped.astype(jnp.float32), axis=0)
    weight_grads = shares.astype(jnp.bfloat16)
    back_grad, back_gate = (
        lax.all_to_all(
            slot_part.reshape(members, capacity, model_width),
            "expert",
            split_axis=0,
            concat_axis=0,
            tiled=True,
        ),
        lax.all_to_all(
            gate_part.reshape(members, capacity), "expert", split_axis=0, concat_axis=0, tiled=True
        ),
    )
    tiled = jnp.broadcast_to(
        place_bf.reshape(experts, 1, capacity, tok_rows), (experts, GROUP, capacity, tok_rows)
    )
    tiled = tiled.reshape(members * capacity, tok_rows)
    grad_tokens = lax.dot_general(
        tiled,
        back_grad.reshape(members * capacity, model_width),
        contract_rows,
        preferred_element_type=jnp.float32,
    ).astype(jnp.bfloat16)
    gate_sum = jnp.sum(
        back_gate.reshape(experts, GROUP, capacity).astype(jnp.float32), axis=1
    ).reshape(slot_count)
    grad_gates = jnp.where(slot_ids >= 0, jnp.take(gate_sum, jnp.maximum(slot_ids, 0), axis=0), 0.0)
    return (
        grad_tokens,
        grad_gates,
        weight_grads[None, :, 0, :],
        weight_grads[None, :, 1, :],
        weight_grads[None, :, 2, :],
    )


def solution(mesh):
    in_specs = (
        P(("expert", "dp"), None),
        P(("expert", "dp"), None),
        P(("expert", "dp"), None),
        P(("expert", "dp"), None),
        P("expert", "dp", None),
        P("expert", "dp", None),
        P("expert", "dp", None),
    )
    out_specs = (
        P(("expert", "dp"), None),
        P(("expert", "dp"), None),
        P("expert", "dp", None),
        P("expert", "dp", None),
        P("expert", "dp", None),
    )
    return jax.shard_map(
        per_device, mesh=mesh, in_specs=in_specs, out_specs=out_specs, check_vma=False
    )
```

profile of v0, /device:TPU:105, one launch (start us, length us, event | category | flops | bytes accessed | tf_op | source)
XLA Modules:
  0.0 467.6 jit_solution(2741525155790413076)
XLA Ops:
  5.2 14.4 %all-to-all-start = ((bf16[32,1,16]{2,1,0:T(2,128)(2,1)}), bf16[32,1,16]{2,1,0:T(2,128)(2,1)S(1)}, u32[]{:S(2)}, u32[]{:S(2)}) async-start(bf16[32,1,16]{2,1,0:T(2,128)(2,1)} %copy.62), calls=%async_computation | async-start | bytes 32768 | tf_op jit(solution)/shard_map/all_to_all | solution.py:74
  20.0 4.9 %all-to-all-done = bf16[32,1,16]{2,1,0:T(2,128)(2,1)S(1)} async-done(((bf16[32,1,16]{2,1,0:T(2,128)(2,1)}), bf16[32,1,16]{2,1,0:T(2,128)(2,1)S(1)}, u32[]{:S(2)}, u32[]{:S(2)}) %all-to-all-start) | async-done | bytes 1056 | tf_op jit(solution)/shard_map/all_to_all | solution.py:74
  26.7 9.7 %all-to-all-start.2 = ((bf16[32,16,2560]{2,1,0:T(8,128)(2,1)}), bf16[32,16,2560]{2,1,0:T(8,128)(2,1)S(1)}, u32[]{:S(2)}, u32[]{:S(2)}) async-start(bf16[32,16,2560]{2,1,0:T(8,128)(2,1)} %bitcast.108), calls=%async_computation.2 | async-start | bytes 5242880 | tf_op jit(solution)/shard_map/all_to_all | solution.py:64
  36.4 2.3 convolution_convert_fusion.5
  38.7 61.4 %all-to-all-done.2 = bf16[32,16,2560]{2,1,0:T(8,128)(2,1)S(1)} async-done(((bf16[32,16,2560]{2,1,0:T(8,128)(2,1)}), bf16[32,16,2560]{2,1,0:T(8,128)(2,1)S(1)}, u32[]{:S(2)}, u32[]{:S(2)}) %all-to-all-start.2) | async-done | bytes 2621472 | tf_op jit(solution)/shard_map/all_to_all | solution.py:64
  100.0 2.9 broadcast_in_dim.79
  102.9 18.5 %all-to-all-start.1 = ((bf16[32,16,2560]{2,1,0:T(8,128)(2,1)}), bf16[32,16,2560]{2,1,0:T(8,128)(2,1)}, u32[]{:S(2)}, u32[]{:S(2)}) async-start(bf16[32,16,2560]{2,1,0:T(8,128)(2,1)} %bitcast.107), calls=%async_computation.1 | async-start | bytes 5242880 | tf_op jit(solution)/shard_map/all_to_all | solution.py:67
  121.8 83.1 %all_gather.9 = bf16[1,192,2560]{2,0,1:T(2,128)(2,1)} all-gather(bf16[1,12,2560]{2,0,1:T(2,128)(2,1)S(1)} %copy.63), channel_id=1, replica_groups=mesh['expert'=32,'dp'=16] {'dp'}, dimensions={1}, use_global_device_ids=true | all-gather | bytes 1044480 | tf_op jit(solution)/shard_map/all_gather | solution.py:89
  204.9 30.5 %all_gather.10 = bf16[1,192,2560]{2,0,1:T(2,128)(2,1)S(1)} all-gather(bf16[1,12,2560]{2,0,1:T(2,128)(2,1)S(1)} %copy.64), channel_id=1, replica_groups=mesh['expert'=32,'dp'=16] {'dp'}, dimensions={1}, use_global_device_ids=true | all-gather | bytes 1044480 | tf_op jit(solution)/shard_map/all_gather | solution.py:88
  235.4 30.0 %all_gather.11 = bf16[1,192,2560]{2,0,1:T(2,128)(2,1)} all-gather(bf16[1,12,2560]{2,0,1:T(2,128)(2,1)S(1)} %copy.65), channel_id=1, replica_groups=mesh['expert'=32,'dp'=16] {'dp'}, dimensions={1}, use_global_device_ids=true | all-gather | bytes 1044480 | tf_op jit(solution)/shard_map/all_gather | solution.py:87
  267.2 2.4 multiply_convert_fusion
  272.1 1.9 fusion.19
  274.1 3.3 fusion.4
  277.4 2.7 fusion
  280.9 24.3 %all-to-all-start.4 = ((bf16[32,1,16]{2,1,0:T(2,128)(2,1)}), bf16[32,1,16]{2,1,0:T(2,128)(2,1)S(1)}, u32[]{:S(2)}, u32[]{:S(2)}) async-start(bf16[32,1,16]{2,1,0:T(2,128)(2,1)} %convert_element_type.144), calls=%async_computation.4 | async-start | bytes 32768 | tf_op jit(solution)/shard_map/all_to_all | solution.py:119
  305.1 5.8 %add_convert_fusion = bf16[512,2560]{1,0:T(8,128)(2,1)} fusion(f32[512,2560]{1,0:T(8,128)} %fusion.4, bf16[1,192,2560]{2,0,1:T(2,128)(2,1)} %copy-done.4, f32[512,192]{0,1:T(8,128)} %copy-done.6, f32[512,192]{0,1:T(8,128)} %copy-done.7), kind=kOutput, calls=%fused_computation.3 | convolution fusion | flops 506527744 | bytes 9633792 | tf_op jit(solution)/shard_map/dot_general | solution.py:35
  311.5 11.7 %all-to-all-start.3 = ((bf16[32,16,2560]{2,1,0:T(8,128)(2,1)}), bf16[32,16,2560]{2,1,0:T(8,128)(2,1)}, u32[]{:S(2)}, u32[]{:S(2)}) async-start(bf16[32,16,2560]{2,1,0:T(8,128)(2,1)} %bitcast.104), calls=%async_computation.3 | async-start | bytes 5242880 | tf_op jit(solution)/shard_map/all_to_all | solution.py:112
  331.1 3.6 copy.72
  334.8 54.7 %all-to-all-done.3 = bf16[32,16,2560]{2,1,0:T(8,128)(2,1)} async-done(((bf16[32,16,2560]{2,1,0:T(8,128)(2,1)}), bf16[32,16,2560]{2,1,0:T(8,128)(2,1)}, u32[]{:S(2)}, u32[]{:S(2)}) %all-to-all-start.3) | async-done | bytes 2621472 | tf_op jit(solution)/shard_map/all_to_all | solution.py:112
  389.4 28.3 %all-to-all-start.5 = ((bf16[16,12,3,2560]{3,1,2,0:T(8,128)(2,1)}), bf16[16,12,3,2560]{3,1,2,0:T(8,128)(2,1)}, u32[]{:S(2)}, u32[]{:S(2)}) async-start(bf16[16,12,3,2560]{3,1,2,0:T(8,128)(2,1)} %copy.72), calls=%async_computation.5 | async-start | bytes 7864320 | tf_op jit(solution)/shard_map/all_to_all | solution.py:108
  418.1 1.9 gather_fusion
  420.8 3.1 convolution_convert_fusion.3
  423.9 40.1 %all-to-all-done.5 = bf16[16,12,3,2560]{3,1,2,0:T(8,128)(2,1)} async-done(((bf16[16,12,3,2560]{3,1,2,0:T(8,128)(2,1)}), bf16[16,12,3,2560]{3,1,2,0:T(8,128)(2,1)}, u32[]{:S(2)}, u32[]{:S(2)}) %all-to-all-start.5) | async-done | bytes 2949152 | tf_op jit(solution)/shard_map/all_to_all | solution.py:108
  464.1 2.9 reduce_sum.62
  (79 shorter events, 22.4 us)
Async XLA Ops:
  0.6 19.0 %copy-start = (bf16[128,2560]{1,0:T(8,128)(2,1)S(1)}, bf16[128,2560]{1,0:T(8,128)(2,1)}, u32[]{:S(2)}) copy-start(bf16[128,2560]{1,0:T(8,128)(2,1)} %param.7) | copy-start | bytes 1966084
  4.4 15.2 %copy-start.15 = (s32[128,2]{0,1:T(2,128)}, s32[128,2]{0,1:T(2,128)S(1)}, u32[]{:S(2)}) copy-start(s32[128,2]{0,1:T(2,128)S(1)} %get-tuple-element.21) | copy-start | bytes 3076
  5.2 19.7 %all-to-all-start = ((bf16[32,1,16]{2,1,0:T(2,128)(2,1)}), bf16[32,1,16]{2,1,0:T(2,128)(2,1)S(1)}, u32[]{:S(2)}, u32[]{:S(2)}) async-start(bf16[32,1,16]{2,1,0:T(2,128)(2,1)} %copy.62), calls=%async_computation | async-start | bytes 32768 | tf_op jit(solution)/shard_map/all_to_all | solution.py:74
  26.7 73.3 %all-to-all-start.2 = ((bf16[32,16,2560]{2,1,0:T(8,128)(2,1)}), bf16[32,16,2560]{2,1,0:T(8,128)(2,1)S(1)}, u32[]{:S(2)}, u32[]{:S(2)}) async-start(bf16[32,16,2560]{2,1,0:T(8,128)(2,1)} %bitcast.108), calls=%async_computation.2 | async-start | bytes 5242880 | tf_op jit(solution)/shard_map/all_to_all | solution.py:64
  102.9 18.6 %copy-start.10 = (bf16[1,12,2560]{2,1,0:T(8,128)(2,1)S(1)}, bf16[1,12,2560]{2,1,0:T(8,128)(2,1)}, u32[]{:S(2)}) copy-start(bf16[1,12,2560]{2,1,0:T(8,128)(2,1)} %param.11) | copy-start | bytes 184324
  102.9 18.7 %copy-start.11 = (bf16[1,12,2560]{2,1,0:T(8,128)(2,1)S(1)}, bf16[1,12,2560]{2,1,0:T(8,128)(2,1)}, u32[]{:S(2)}) copy-start(bf16[1,12,2560]{2,1,0:T(8,128)(2,1)} %param.12) | copy-start | bytes 184324
  102.9 18.8 %copy-start.12 = (bf16[1,12,2560]{2,1,0:T(8,128)(2,1)S(1)}, bf16[1,12,2560]{2,1,0:T(8,128)(2,1)}, u32[]{:S(2)}) copy-start(bf16[1,12,2560]{2,1,0:T(8,128)(2,1)} %param.13) | copy-start | bytes 184324
  102.9 164.3 %all-to-all-start.1 = ((bf16[32,16,2560]{2,1,0:T(8,128)(2,1)}), bf16[32,16,2560]{2,1,0:T(8,128)(2,1)}, u32[]{:S(2)}, u32[]{:S(2)}) async-start(bf16[32,16,2560]{2,1,0:T(8,128)(2,1)} %bitcast.107), calls=%async_computation.1 | async-start | bytes 5242880 | tf_op jit(solution)/shard_map/all_to_all | solution.py:67
  235.4 30.0 %copy-start.4 = (bf16[1,192,2560]{2,0,1:T(2,128)(2,1)}, bf16[1,192,2560]{2,0,1:T(2,128)(2,1)S(1)}, u32[]{:S(2)}) copy-start(bf16[1,192,2560]{2,0,1:T(2,128)(2,1)S(1)} %all_gather.10) | copy-start | bytes 2949124
  267.2 2.4 copy-start.5
  269.6 1.5 copy-start.1
  269.6 2.5 copy-start.3
  269.6 2.5 copy-start.9
  272.1 1.9 copy-start.6
  274.1 3.3 copy-start.7
  280.9 30.0 %all-to-all-start.4 = ((bf16[32,1,16]{2,1,0:T(2,128)(2,1)}), bf16[32,1,16]{2,1,0:T(2,128)(2,1)S(1)}, u32[]{:S(2)}, u32[]{:S(2)}) async-start(bf16[32,1,16]{2,1,0:T(2,128)(2,1)} %convert_element_type.144), calls=%async_computation.4 | async-start | bytes 32768 | tf_op jit(solution)/shard_map/all_to_all | solution.py:119
  310.9 0.6 copy-start.13
  311.5 77.9 %all-to-all-start.3 = ((bf16[32,16,2560]{2,1,0:T(8,128)(2,1)}), bf16[32,16,2560]{2,1,0:T(8,128)(2,1)}, u32[]{:S(2)}, u32[]{:S(2)}) async-start(bf16[32,16,2560]{2,1,0:T(8,128)(2,1)} %bitcast.104), calls=%async_computation.3 | async-start | bytes 5242880 | tf_op jit(solution)/shard_map/all_to_all | solution.py:112
  326.6 1.7 copy-start.8
  328.3 1.7 copy-start.2
  334.8 83.0 %copy-start.17 = (s32[128,2]{0,1:T(2,128)S(1)}, s32[128,2]{0,1:T(2,128)}, u32[]{:S(2)}) copy-start(s32[128,2]{0,1:T(2,128)} %get-tuple-element.20) | copy-start | bytes 3076
  334.8 83.2 %copy-start.14 = (bf16[32,1,16]{2,1,0:T(2,128)(2,1)S(1)}, bf16[32,1,16]{2,1,0:T(2,128)(2,1)}, u32[]{:S(2)}) copy-start(bf16[32,1,16]{2,1,0:T(2,128)(2,1)} %copy-done.13) | copy-start | bytes 3076
  389.4 74.7 %all-to-all-start.5 = ((bf16[16,12,3,2560]{3,1,2,0:T(8,128)(2,1)}), bf16[16,12,3,2560]{3,1,2,0:T(8,128)(2,1)}, u32[]{:S(2)}, u32[]{:S(2)}) async-start(bf16[16,12,3,2560]{3,1,2,0:T(8,128)(2,1)} %copy.72), calls=%async_computation.5 | async-start | bytes 7864320 | tf_op jit(solution)/shard_map/all_to_all | solution.py:108
  418.1 2.1 copy-start.16
where the time goes:
time: 469 us; the launch traced here: 468 us
  waiting for transfers between devices  161 us (34%)
  blocking collectives  144 us (31%)
  starting transfers between devices  107 us (23%)
  matrix products  25.3 us (5%)
  local copies, waits for them, and re-layouts  19.9 us (4%)
  other arithmetic  9.89 us (2%)
    all_gather x1, blocking collectives, per_device(): lax.all_gather(down_proj, 'dp', axis=1, tiled=True)  83.1 us
    all_to_all x1, waiting for transfers between devices, per_device(): lax.all_to_all(spread_out(sent_x, experts, capacity), 'expert', split_axi...  61.4 us
    all_to_all x1, waiting for transfers between devices, per_device(): lax.all_to_all(slot_part.reshape(members, capacity, model_width), 'expert...  54.7 us
    all_to_all x1, waiting for transfers between devices, per_device(): lax.all_to_all(parted, 'dp', split_axis=0, concat_axis=0, tiled=True)  40.1 us
    all_gather x1, blocking collectives, per_device(): lax.all_gather(up_proj, 'dp', axis=1, tiled=True)  30.5 us
    all_gather x1, blocking collectives, per_device(): lax.all_gather(gate_proj, 'dp', axis=1, tiled=True)  30 us
    all_to_all x1, starting transfers between devices, per_device(): lax.all_to_all(parted, 'dp', split_axis=0, concat_axis=0, tiled=True)  28.3 us
    all_to_all x1, starting transfers between devices, per_device(): lax.all_to_all(gate_part.reshape(members, capacity), 'expert', split_axis...  24.3 us
  transfers between devices with their start and end apart: 6, of which 4 were waited for; matrix products, arithmetic and copies ran while one was open for 6% of the time, Pallas kernels for 0%

commit v1 on v0

--- a/solution.py
+++ b/solution.py
@@ -84,7 +84,9 @@
     rows_gate = got_gate.reshape(-1).astype(jnp.float32)
     scaled_dy = (rows_gate[:, None] * rows_dy.astype(jnp.float32)).astype(jnp.bfloat16)
     full_gate, full_up, full_down = (
-        lax.all_gather(gate_proj, "dp", axis=1, tiled=True),
+        jnp.concatenate(
+            lax.all_to_all(jnp.stack([gate_proj] * lax.axis_size("dp")), "dp", 0, 0), axis=1
+        ),
         lax.all_gather(up_proj, "dp", axis=1, tiled=True),
         lax.all_gather(down_proj, "dp", axis=1, tiled=True),
     )

time: 469 us -> 494 us (1.053)
  the two profiles are of different devices: /device:TPU:105 before, /device:TPU:121 now
where the time goes in v1:
time: 494 us; the launch traced here: 493 us
  waiting for transfers between devices  204 us (41%)
  blocking collectives  150 us (30%)
  starting transfers between devices  78.1 us (16%)
  matrix products  26.9 us (5%)
  local copies, waits for them, and re-layouts  23.2 us (5%)
  other arithmetic  9.89 us (2%)
    all_gather x1, blocking collectives, per_device(): lax.all_gather(down_proj, 'dp', axis=1, tiled=True)  94.6 us
    all_to_all x1, waiting for transfers between devices, per_device(): lax.all_to_all(slot_part.reshape(members, capacity, model_width), 'expert...  85.8 us
    all_to_all x1, waiting for transfers between devices, per_device(): lax.all_to_all(spread_out(sent_x, experts, capacity), 'expert', split_axi...  60.4 us
    all_to_all x1, waiting for transfers between devices, per_device(): lax.all_to_all(parted, 'dp', split_axis=0, concat_axis=0, tiled=True)  39.2 us
    all_gather x1, blocking collectives, per_device(): lax.all_gather(up_proj, 'dp', axis=1, tiled=True)  34.1 us
    all_to_all x1, starting transfers between devices, per_device(): lax.all_to_all(gate_part.reshape(members, capacity), 'expert', split_axis...  33.7 us
    all_to_all x1, blocking collectives, per_device(): lax.all_to_all(spread_out(sent_gate, experts, capacity), 'expert', split_...  21 us
    all_to_all x1, waiting for transfers between devices, per_device(): lax.all_to_all(jnp.stack([gate_proj] * lax.axis_size('dp')), 'dp', 0, 0)  17.8 us
  transfers between devices with their start and end apart: 6, of which 5 were waited for; matrix products, arithmetic and copies ran while one was open for 6% of the time, Pallas kernels for 0%

profile of v1, /device:TPU:121, one launch (start us, length us, event | category | flops | bytes accessed | tf_op | source)
XLA Modules:
  0.0 493.3 jit_solution(1068791060486408771)
XLA Ops:
  4.6 21.0 %all_to_all.40 = bf16[32,1,16]{2,1,0:T(2,128)(2,1)S(1)} all-to-all(bf16[32,1,16]{2,1,0:T(2,128)(2,1)S(1)} %copy.60), channel_id=1, replica_groups=mesh['expert'=32,'dp'=16] {'expert'}, dimensions={0} | all-to-all | bytes 2048 | tf_op jit(solution)/shard_map/all_to_all | solution.py:74
  27.7 7.5 %all-to-all-start.3 = ((bf16[16,1,12,2560]{3,2,1,0:T(8,128)(2,1)}), bf16[16,1,12,2560]{3,2,1,0:T(8,128)(2,1)S(1)}, u32[]{:S(2)}, u32[]{:S(2)}) async-start(bf16[16,1,12,2560]{3,2,1,0:T(8,128)(2,1)} %stack.4), calls=%async_computation.3 | async-start | bytes 2621440 | tf_op jit(solution)/shard_map/all_to_all | solution.py:88
  35.6 17.8 %all-to-all-done.3 = bf16[16,1,12,2560]{3,2,1,0:T(8,128)(2,1)S(1)} async-done(((bf16[16,1,12,2560]{3,2,1,0:T(8,128)(2,1)}), bf16[16,1,12,2560]{3,2,1,0:T(8,128)(2,1)S(1)}, u32[]{:S(2)}, u32[]{:S(2)}) %all-to-all-start.3) | async-done | bytes 983072 | tf_op jit(solution)/shard_map/all_to_all | solution.py:88
  55.3 8.1 %all-to-all-start.2 = ((bf16[32,16,2560]{2,1,0:T(8,128)(2,1)}), bf16[32,16,2560]{2,1,0:T(8,128)(2,1)S(1)}, u32[]{:S(2)}, u32[]{:S(2)}) async-start(bf16[32,16,2560]{2,1,0:T(8,128)(2,1)} %bitcast.104), calls=%async_computation.2 | async-start | bytes 5242880 | tf_op jit(solution)/shard_map/all_to_all | solution.py:64
  63.4 2.3 convolution_convert_fusion.5
  65.6 60.4 %all-to-all-done.2 = bf16[32,16,2560]{2,1,0:T(8,128)(2,1)S(1)} async-done(((bf16[32,16,2560]{2,1,0:T(8,128)(2,1)}), bf16[32,16,2560]{2,1,0:T(8,128)(2,1)S(1)}, u32[]{:S(2)}, u32[]{:S(2)}) %all-to-all-start.2) | async-done | bytes 2621472 | tf_op jit(solution)/shard_map/all_to_all | solution.py:64
  126.0 2.9 broadcast_in_dim.79
  129.0 13.8 %all-to-all-start.1 = ((bf16[32,16,2560]{2,1,0:T(8,128)(2,1)}), bf16[32,16,2560]{2,1,0:T(8,128)(2,1)}, u32[]{:S(2)}, u32[]{:S(2)}) async-start(bf16[32,16,2560]{2,1,0:T(8,128)(2,1)} %bitcast.103), calls=%async_computation.1 | async-start | bytes 5242880 | tf_op jit(solution)/shard_map/all_to_all | solution.py:67
  143.0 94.6 %all_gather.6 = bf16[1,192,2560]{2,0,1:T(2,128)(2,1)} all-gather(bf16[1,12,2560]{2,0,1:T(2,128)(2,1)S(1)} %copy.61), channel_id=1, replica_groups=mesh['expert'=32,'dp'=16] {'dp'}, dimensions={1}, use_global_device_ids=true | all-gather | bytes 1044480 | tf_op jit(solution)/shard_map/all_gather | solution.py:91
  237.7 34.1 %all_gather.7 = bf16[1,192,2560]{2,0,1:T(2,128)(2,1)} all-gather(bf16[1,12,2560]{2,0,1:T(2,128)(2,1)S(1)} %copy.62), channel_id=1, replica_groups=mesh['expert'=32,'dp'=16] {'dp'}, dimensions={1}, use_global_device_ids=true | all-gather | bytes 1044480 | tf_op jit(solution)/shard_map/all_gather | solution.py:90
  271.8 2.2 squeeze_reshape.3
  274.1 3.3 fusion.5
  277.4 2.4 multiply_convert_fusion
  284.0 3.3 fusion.24
  287.2 2.7 fusion
  290.7 33.7 %all-to-all-start.5 = ((bf16[32,1,16]{2,1,0:T(2,128)(2,1)}), bf16[32,1,16]{2,1,0:T(2,128)(2,1)S(1)}, u32[]{:S(2)}, u32[]{:S(2)}) async-start(bf16[32,1,16]{2,1,0:T(2,128)(2,1)} %convert_element_type.144), calls=%async_computation.5 | async-start | bytes 32768 | tf_op jit(solution)/shard_map/all_to_all | solution.py:121
  324.4 5.8 %add_convert_fusion = bf16[512,2560]{1,0:T(8,128)(2,1)} fusion(f32[512,2560]{1,0:T(8,128)} %fusion.24, bf16[1,192,2560]{2,0,1:T(2,128)(2,1)} %all_gather.7, f32[512,192]{0,1:T(8,128)} %copy-done.5, f32[512,192]{0,1:T(8,128)} %copy-done.6), kind=kOutput, calls=%fused_computation.3 | convolution fusion | flops 506527744 | bytes 9633792 | tf_op jit(solution)/shard_map/dot_general | solution.py:35
  332.0 10.6 %all-to-all-start.4 = ((bf16[32,16,2560]{2,1,0:T(8,128)(2,1)}), bf16[32,16,2560]{2,1,0:T(8,128)(2,1)}, u32[]{:S(2)}, u32[]{:S(2)}) async-start(bf16[32,16,2560]{2,1,0:T(8,128)(2,1)} %bitcast.100), calls=%async_computation.4 | async-start | bytes 5242880 | tf_op jit(solution)/shard_map/all_to_all | solution.py:114
  350.4 3.5 copy.69
  354.0 85.8 %all-to-all-done.4 = bf16[32,16,2560]{2,1,0:T(8,128)(2,1)} async-done(((bf16[32,16,2560]{2,1,0:T(8,128)(2,1)}), bf16[32,16,2560]{2,1,0:T(8,128)(2,1)}, u32[]{:S(2)}, u32[]{:S(2)}) %all-to-all-start.4) | async-done | bytes 2621472 | tf_op jit(solution)/shard_map/all_to_all | solution.py:114
  439.8 4.4 all-to-all-start.6
  447.4 3.1 convolution_convert_fusion.3
  450.5 39.2 %all-to-all-done.6 = bf16[16,12,3,2560]{3,1,2,0:T(8,128)(2,1)} async-done(((bf16[16,12,3,2560]{3,1,2,0:T(8,128)(2,1)}), bf16[16,12,3,2560]{3,1,2,0:T(8,128)(2,1)}, u32[]{:S(2)}, u32[]{:S(2)}) %all-to-all-start.6) | async-done | bytes 2949152 | tf_op jit(solution)/shard_map/all_to_all | solution.py:110
  489.7 2.9 reduce_sum.62
  (78 shorter events, 26.7 us)
Async XLA Ops:
  0.6 34.6 %copy-start = (bf16[128,2560]{1,0:T(8,128)(2,1)S(1)}, bf16[128,2560]{1,0:T(8,128)(2,1)}, u32[]{:S(2)}) copy-start(bf16[128,2560]{1,0:T(8,128)(2,1)} %param.7) | copy-start | bytes 1966084
  4.4 31.2 %copy-start.14 = (s32[128,2]{0,1:T(2,128)}, s32[128,2]{0,1:T(2,128)S(1)}, u32[]{:S(2)}) copy-start(s32[128,2]{0,1:T(2,128)S(1)} %get-tuple-element.21) | copy-start | bytes 3076
  27.7 25.7 %all-to-all-start.3 = ((bf16[16,1,12,2560]{3,2,1,0:T(8,128)(2,1)}), bf16[16,1,12,2560]{3,2,1,0:T(8,128)(2,1)S(1)}, u32[]{:S(2)}, u32[]{:S(2)}) async-start(bf16[16,1,12,2560]{3,2,1,0:T(8,128)(2,1)} %stack.4), calls=%async_computation.3 | async-start | bytes 2621440 | tf_op jit(solution)/shard_map/all_to_all | solution.py:88
  53.4 1.9 copy-start.3
  55.3 70.7 %all-to-all-start.2 = ((bf16[32,16,2560]{2,1,0:T(8,128)(2,1)}), bf16[32,16,2560]{2,1,0:T(8,128)(2,1)S(1)}, u32[]{:S(2)}, u32[]{:S(2)}) async-start(bf16[32,16,2560]{2,1,0:T(8,128)(2,1)} %bitcast.104), calls=%async_computation.2 | async-start | bytes 5242880 | tf_op jit(solution)/shard_map/all_to_all | solution.py:64
  129.0 13.8 %copy-start.10 = (bf16[1,12,2560]{2,1,0:T(8,128)(2,1)S(1)}, bf16[1,12,2560]{2,1,0:T(8,128)(2,1)}, u32[]{:S(2)}) copy-start(bf16[1,12,2560]{2,1,0:T(8,128)(2,1)} %param.12) | copy-start | bytes 184324
  129.0 14.0 %copy-start.11 = (bf16[1,12,2560]{2,1,0:T(8,128)(2,1)S(1)}, bf16[1,12,2560]{2,1,0:T(8,128)(2,1)}, u32[]{:S(2)}) copy-start(bf16[1,12,2560]{2,1,0:T(8,128)(2,1)} %param.13) | copy-start | bytes 184324
  129.0 148.4 %all-to-all-start.1 = ((bf16[32,16,2560]{2,1,0:T(8,128)(2,1)}), bf16[32,16,2560]{2,1,0:T(8,128)(2,1)}, u32[]{:S(2)}, u32[]{:S(2)}) async-start(bf16[32,16,2560]{2,1,0:T(8,128)(2,1)} %bitcast.103), calls=%async_computation.1 | async-start | bytes 5242880 | tf_op jit(solution)/shard_map/all_to_all | solution.py:67
  277.4 2.4 copy-start.7
  279.8 1.5 copy-start.1
  279.8 1.9 copy-start.4
  279.8 2.2 copy-start.8
  282.0 2.0 copy-start.5
  284.0 3.3 copy-start.6
  290.7 40.7 %all-to-all-start.5 = ((bf16[32,1,16]{2,1,0:T(2,128)(2,1)}), bf16[32,1,16]{2,1,0:T(2,128)(2,1)S(1)}, u32[]{:S(2)}, u32[]{:S(2)}) async-start(bf16[32,1,16]{2,1,0:T(2,128)(2,1)} %convert_element_type.144), calls=%async_computation.5 | async-start | bytes 32768 | tf_op jit(solution)/shard_map/all_to_all | solution.py:121
  331.4 0.6 copy-start.12
  332.0 107.8 %all-to-all-start.4 = ((bf16[32,16,2560]{2,1,0:T(8,128)(2,1)}), bf16[32,16,2560]{2,1,0:T(8,128)(2,1)}, u32[]{:S(2)}, u32[]{:S(2)}) async-start(bf16[32,16,2560]{2,1,0:T(8,128)(2,1)} %bitcast.100), calls=%async_computation.4 | async-start | bytes 5242880 | tf_op jit(solution)/shard_map/all_to_all | solution.py:114
  345.9 1.7 copy-start.9
  347.7 1.7 copy-start.2
  354.0 90.3 %copy-start.16 = (s32[128,2]{0,1:T(2,128)S(1)}, s32[128,2]{0,1:T(2,128)}, u32[]{:S(2)}) copy-start(s32[128,2]{0,1:T(2,128)} %get-tuple-element.20) | copy-start | bytes 3076
  354.0 90.6 %copy-start.13 = (bf16[32,1,16]{2,1,0:T(2,128)(2,1)S(1)}, bf16[32,1,16]{2,1,0:T(2,128)(2,1)}, u32[]{:S(2)}) copy-start(bf16[32,1,16]{2,1,0:T(2,128)(2,1)} %copy-done.12) | copy-start | bytes 3076
  439.8 49.9 %all-to-all-start.6 = ((bf16[16,12,3,2560]{3,1,2,0:T(8,128)(2,1)}), bf16[16,12,3,2560]{3,1,2,0:T(8,128)(2,1)}, u32[]{:S(2)}, u32[]{:S(2)}) async-start(bf16[16,12,3,2560]{3,1,2,0:T(8,128)(2,1)} %copy.69), calls=%async_computation.6 | async-start | bytes 7864320 | tf_op jit(solution)/shard_map/all_to_all | solution.py:110
  444.7 2.1 copy-start.15
